TPU v7x, 32 devices: a whole 2x2x4 slice. The times are simulated.
32 devices in a mesh: ha: 8 (over y, x, core), wa: 4 (over z).
Axes of the slice: x: 2, y: 2, z: 4, core: 2. Of those that a mesh axis runs over, the one named last changes fastest.
Arguments:
- features: bfloat16 [1, 256, 256, 256], P(None, 'ha', 'wa'), may hold values from -6 to 6
- cotangent: bfloat16 [1, 256, 256, 256], P(None, 'ha', 'wa'), may hold values from -6 to 6
- qkv_weight: bfloat16 [256, 768], replicated, may hold values from -0.375 to 0.375
- out_weight: bfloat16 [256, 256], replicated, may hold values from -0.375 to 0.375
- up_weight: bfloat16 [256, 1024], replicated, may hold values from -0.375 to 0.375
- down_weight: bfloat16 [1024, 256], replicated, may hold values from -0.1875 to 0.1875
- norm_gains: float32 [2, 256], replicated, may hold values from 0.5 to 1.5
Outputs:
- grad_input: bfloat16 [1, 256, 256, 256], P(None, 'ha', 'wa')
- grad_qkv: float32 [256, 768], replicated
- grad_out: float32 [256, 256], replicated
- grad_up: float32 [256, 1024], replicated
- grad_down: float32 [1024, 256], replicated
- grad_gains: float32 [2, 256], replicated
All inputs are finite; a program needn't handle non-finite values.
Results may differ from a plain program's by a relative error of at most 0.012.
Values may be sent and summed in bfloat16 or wider, within the bound.
A program may use at most 128 MiB of HBM per device.

v0:
```python
import functools
import math

import jax
import jax.numpy as jnp
from jax import lax
from jax.experimental import pallas as pl
from jax.experimental.pallas import tpu as pltpu
from jax.sharding import PartitionSpec as P

HEADS = 8
GRID = 8
EPS = 1e-05
LANES = 128
ROWS = 16
BF = jnp.bfloat16
F32 = jnp.float32


def mm(a, b, ca=1, cb=0):
    return lax.dot_general(a, b, (((ca,), (cb,)), ((), ())), preferred_element_type=F32)


def norm_forward(values, gain):
    centre = values - jnp.mean(values, axis=-1, keepdims=True)
    scaled = lax.rsqrt(jnp.mean(centre * centre, axis=-1, keepdims=True) + EPS)
    return centre * scaled, scaled


def norm_backward(grad, normed, scaled, gain):
    inner = grad * gain
    first = jnp.mean(inner, axis=-1, keepdims=True)
    second = jnp.mean(inner * normed, axis=-1, keepdims=True)
    return scaled * (inner - first - normed * second)


def head_masks(members, head_dim):
    lane = lax.broadcasted_iota(jnp.int32, (members, LANES), 1) // head_dim
    return [lane == h for h in range(LANES // head_dim)]


def spread(part, masks):
    zero = jnp.zeros_like(part)
    return jnp.concatenate([jnp.where(m, part, zero) for m in masks], axis=0)


def collect(blocks, masks, members):
    out = blocks[:members]
    for h in range(1, len(masks)):
        out = jnp.where(masks[h], blocks[h * members : (h + 1) * members], out)
    return out


def chunk_work(
    load_in, load_cot, store_out, first,
    wqkv, wout, wup, wdown, gains,
    a_qkv, a_out, a_up, a_down, a_gains,
    reg, qkv, probs, mid, rows_out,
):
    rows, channels = mid.shape
    members = GRID * GRID
    head_dim = channels // HEADS
    groups = rows // members
    halves = channels // LANES
    scale = head_dim ** (-0.5)
    masks = head_masks(members, head_dim)
    per_half = len(masks)
    wide = per_half * members

    def add_to(ref, index, value):
        ref[index] = ref[index] + value

    def grouped(load):
        flat = load().astype(F32)
        for half in range(halves):
            reg[half] = flat[:, half * LANES : (half + 1) * LANES]
        return jnp.concatenate(
            [
                jnp.concatenate(
                    [reg[half, pl.ds(j, members, stride=groups), :] for half in range(halves)],
                    axis=1,
                )
                for j in range(groups)
            ],
            axis=0,
        )

    gain_a, gain_b = gains[0:1, :], gains[1:2, :]
    cot = grouped(load_cot)
    cot_low = cot.astype(BF)
    values = grouped(load_in)
    normed_a, scaled_a = norm_forward(values, gain_a)
    input_norm = (normed_a * gain_a).astype(BF)
    qkv[...] = mm(input_norm, wqkv[...]).astype(BF)

    def section(g, which, half):
        start = which * channels + half * LANES
        return qkv[g * members : (g + 1) * members, start : start + LANES]

    for g in range(groups):
        for half in range(halves):
            q, k, v = (section(g, which, half) for which in range(3))
            e = jnp.exp(mm(k, spread(q, masks), 1, 1) * scale)
            p = e / jnp.sum(e, axis=0, keepdims=True)
            probs[g, half] = p
            ctx = collect(mm(p.astype(BF), v, 0, 0), masks, members)
            mid[g * members : (g + 1) * members, half * LANES : (half + 1) * LANES] = ctx.astype(BF)

    context = mid[...]
    hidden = (values + mm(context, wout[...])).astype(BF).astype(F32)
    normed_b, scaled_b = norm_forward(hidden, gain_b)
    mid_norm = (normed_b * gain_b).astype(BF)
    root = math.sqrt(2.0 / math.pi)
    grad_mid = None
    width = 256
    for start in range(0, wup.shape[1], width):
        cols = slice(start, start + width)
        pre = mm(mid_norm, wup[:, cols])
        square = pre * pre
        t = jnp.tanh(root * (pre + 0.044715 * (square * pre)))
        half_up = 0.5 * (1.0 + t)
        act = (pre * half_up).astype(BF)
        slope = half_up + (0.5 * root) * pre * (1.0 - t * t) * (1.0 + (3 * 0.044715) * square)
        grad_pre = (mm(cot_low, wdown[cols, :], 1, 1) * slope).astype(BF)
        add_to(a_down, (slice(None), cols), mm(cot_low, act, 0, 0))
        add_to(a_up, (slice(None), cols), mm(mid_norm, grad_pre, 0, 0))
        part = mm(grad_pre, wup[:, cols], 1, 1)
        grad_mid = part if grad_mid is None else grad_mid + part
    add_to(a_gains, (slice(1, 2), slice(None)), jnp.sum(grad_mid * normed_b, axis=0, keepdims=True))
    grad_hidden = (cot + norm_backward(grad_mid, normed_b, scaled_b, gain_b)).astype(BF)
    add_to(a_out, Ellipsis, mm(context, grad_hidden, 0, 0))
    mid[...] = mm(grad_hidden, wout[...], 1, 1).astype(BF)

    for g in range(groups):
        at = slice(g * members, (g + 1) * members)
        for half in range(halves):
            q, k, v = (section(g, which, half) for which in range(3))
            p = probs[g, half]
            gc = spread(mid[at, half * LANES : (half + 1) * LANES], masks)
            gp = mm(v, gc, 1, 1)
            gs = (p * (gp - jnp.sum(p * gp, axis=0, keepdims=True)) * scale).astype(BF)
            grads = (
                collect(mm(gs, k, 0, 0), masks, members),
                mm(gs, spread(q, masks)),
                mm(p.astype(BF), gc),
            )
            for which in range(3):
                begin = which * channels + half * LANES
                rows_out[at, begin : begin + LANES] = grads[which].astype(BF)

    grad_rows = rows_out[...]
    add_to(a_qkv, Ellipsis, mm(input_norm, grad_rows, 0, 0))
    grad_norm = mm(grad_rows, wqkv[...], 1, 1)
    add_to(a_gains, (slice(0, 1), slice(None)), jnp.sum(grad_norm * normed_a, axis=0, keepdims=True))
    result = grad_hidden.astype(F32) + norm_backward(grad_norm, normed_a, scaled_a, gain_a)
    for half in range(halves):
        for j in range(groups):
            reg[half, pl.ds(j, members, stride=groups), :] = result[
                j * members : (j + 1) * members, half * LANES : (half + 1) * LANES
            ]
    store_out(jnp.concatenate([reg[half] for half in range(halves)], axis=1).astype(BF))


def local_kernel(x_ref, wqkv, wout, wup, wdown, gains, o_ref, *rest):
    sums, scratch = rest[:5], rest[5:]
    peers, _, _, piece, channels = x_ref.shape
    rows = peers * piece

    @pl.when(pl.program_id(0) == 0)
    def _():
        for ref in sums:
            ref[...] = jnp.zeros_like(ref)

    def store(value):
        o_ref[:, 0] = value.reshape(peers, piece, channels)

    chunk_work(
        lambda: x_ref[:, 0, 0].reshape(rows, channels),
        lambda: x_ref[:, 0, 1].reshape(rows, channels),
        store, None, wqkv, wout, wup, wdown, gains, *sums, *scratch,
    )


def scratch_of(rows, channels):
    members = GRID * GRID
    halves = channels // LANES
    wide = (HEADS // halves) * members
    return [
        pltpu.VMEM((halves, rows, LANES), F32),
        pltpu.VMEM((rows, 3 * channels), BF),
        pltpu.VMEM((rows // members, halves, members, wide), F32),
        pltpu.VMEM((rows, channels), BF),
        pltpu.VMEM((rows, 3 * channels), BF),
    ]


def local_call(x, wqkv, wout, wup, wdown, gains):
    peers, chunks, _, piece, channels = x.shape
    hidden = wup.shape[1]

    def whole(shape):
        return pl.BlockSpec(shape, lambda c: (0,) * len(shape))

    sums = [(channels, 3 * channels), (channels, channels), (channels, hidden), (channels, hidden), (2, channels)]
    return pl.pallas_call(
        local_kernel,
        grid=(chunks,),
        in_specs=[pl.BlockSpec((peers, 1, 2, piece, channels), lambda c: (0, c, 0, 0, 0))]
        + [whole(a.shape) for a in (wqkv, wout, wup, wdown, gains)],
        out_specs=[pl.BlockSpec((peers, 1, piece, channels), lambda c: (0, c, 0, 0))]
        + [whole(s) for s in sums],
        out_shape=[jax.ShapeDtypeStruct((peers, chunks, piece, channels), BF)]
        + [jax.ShapeDtypeStruct(s, F32) for s in sums],
        scratch_shapes=scratch_of(peers * piece, channels),
        compiler_params=pltpu.CompilerParams(vmem_limit_bytes=56 << 20),
    )(x, wqkv, wout, wup, wdown, gains)


def layout(rows_dev, cols_dev, tile_rows, tile_cols):
    stride_h = tile_rows * rows_dev // GRID
    stride_w = tile_cols * cols_dev // GRID
    classes = max(1, stride_h // tile_rows)
    assert stride_h == classes * tile_rows and tile_cols % stride_w == 0
    inner = tile_cols // stride_w
    peers = rows_dev // classes * cols_dev
    mine = tile_rows * stride_w // peers
    assert tile_rows * stride_w == mine * peers and stride_w % mine == 0
    per_chunk = ROWS // inner
    assert mine % per_chunk == 0
    return classes, inner, peers, stride_w // mine, mine // per_chunk, per_chunk


def shards(mesh_shape, features, cotangent, qkv_weight, out_weight, up_weight, down_weight, norm_gains):
    images, tile_rows, tile_cols, channels = features.shape
    rows_dev, cols_dev = mesh_shape["ha"], mesh_shape["wa"]
    classes, inner, peers, cuts, chunks, per_chunk = layout(rows_dev, cols_dev, tile_rows, tile_cols)
    split = (tile_rows, inner, cuts, chunks, per_chunk, channels)

    def pack(tile):
        cut = jnp.transpose(tile.reshape(split), (0, 2, 3, 1, 4, 5))
        return cut.reshape(peers, chunks, ROWS, channels)

    def unpack(packed):
        cut = packed.reshape(tile_rows, cuts, chunks, inner, per_chunk, channels)
        return jnp.transpose(cut, (0, 3, 1, 2, 4, 5)).reshape(images, tile_rows, tile_cols, channels)

    def exchange(x):
        if classes == 1:
            return lax.all_to_all(x, ("ha", "wa"), 0, 0, tiled=True)
        everyone = [
            [(h * classes + c) * cols_dev + w for h in range(rows_dev // classes) for w in range(cols_dev)]
            for c in range(classes)
        ]
        return lax.all_to_all(x, ("ha", "wa"), 0, 0, tiled=True, axis_index_groups=everyone)

    arrived = exchange(jnp.stack([pack(features), pack(cotangent)], axis=2))
    done, *sums = local_call(arrived, qkv_weight, out_weight, up_weight, down_weight, norm_gains)
    totals = lax.psum(tuple(sums), ("ha", "wa"))
    grad_input = unpack(exchange(done))
    factor = 1.0 / float(images * tile_rows * tile_cols * rows_dev * cols_dev) ** 0.5
    return (
        grad_input,
        totals[0] * factor,
        totals[1] * factor,
        totals[2] * factor,
        totals[3].T * factor,
        totals[4] * factor,
    )


def solution(mesh):
    return jax.shard_map(
        functools.partial(shards, dict(mesh.shape)),
        mesh=mesh,
        in_specs=(P(None, "ha", "wa", None), P(None, "ha", "wa", None), P(), P(), P(), P(), P()),
        out_specs=(P(None, "ha", "wa", None), P(), P(), P(), P(), P()),
        check_vma=False,
    )
```

profile of v0, /device:TPU:1, one launch (start us, length us, event | category | flops | bytes accessed | tf_op | source)
XLA Modules:
  0.0 277.7 jit_solution(7987460668201370634)
XLA Ops:
  7.2 0.0 all-reduce.3.cloned.1.call-start
  7.2 1.7 copy_bitcast_fusion
  8.9 0.2 pad_maximum_fusion
  9.1 55.8 %all_to_all.10.x_ref = bf16[32,4,2,16,256]{4,3,2,1,0:T(8,128)(2,1)} all-to-all(bf16[32,4,2,16,256]{4,3,2,1,0:T(8,128)(2,1)S(1)} %pad_maximum_fusion), channel_id=1, replica_groups=mesh['ha'=8,'wa'=4] {'ha','wa'}, dimensions={0} | all-to-all | bytes 4194304 | tf_op jit(solution)/shard_map/all_to_all | solution.py:249
  65.0 46.9 %shard_map.118 = (bf16[32,4,16,256]{3,2,1,0:T(8,128)(2,1)}, f32[256,768]{1,0:T(8,128)}, f32[256,256]{1,0:T(8,128)}, f32[256,1024]{1,0:T(8,128)}, f32[256,1024]{1,0:T(8,128)}, /*index=5*/f32[2,256]{1,0:T(2,128)}) custom-call(bf16[32,4,2,16,256]{4,3,2,1,0:T(8,128)(2,1)} %all_to_all.10.x_ref, bf16[256,768]{1,0:T(8,128)(2,1)} %wqkv.1, bf16[256,256]{1,0:T(8,128)(2,1)} %wout.1, ...), custom_call_target="tpu_custom_call" | custom-call | tf_op jit(solution)/shard_map/pallas_call | solution.py:205
  111.9 0.0 copy-start.2
  111.9 0.0 all-reduce.3.cloned.1.call-update
  111.9 3.2 %all-to-all-start.1 = ((bf16[32,4,16,256]{3,2,1,0:T(8,128)(2,1)}), bf16[32,4,16,256]{3,2,1,0:T(8,128)(2,1)S(1)}, u32[]{:S(2)}, u32[]{:S(2)}) async-start(bf16[32,4,16,256]{3,2,1,0:T(8,128)(2,1)} %get-tuple-element.12), calls=%async_computation.1 | async-start | bytes 2097152 | tf_op jit(solution)/shard_map/all_to_all | solution.py:249
  115.1 0.0 copy-done.2
  115.1 57.2 %psum.39 = f32[2,256]{1,0:T(2,128)S(1)} all-reduce(f32[2,256]{1,0:T(2,128)S(1)} %copy-done.2), channel_id=1, replica_groups=mesh['ha'=8,'wa'=4] {'ha','wa'}, use_global_device_ids=true, to_apply=%region_4.0 | all-reduce | flops 512 | bytes 4096 | tf_op jit(solution)/shard_map/psum | solution.py:258
  172.3 0.6 broadcast_multiply_fusion.3
  172.9 90.4 %all-reduce.3.cloned.1.call-done = (f32[256,768]{1,0:T(8,128)}, f32[256,256]{1,0:T(8,128)}, f32[256,1024]{1,0:T(8,128)}, f32[256,1024]{1,0:T(8,128)}) async-done(((f32[256,768]{1,0:T(8,128)}, f32[256,256]{1,0:T(8,128)}, f32[256,1024]{1,0:T(8,128)}, f32[256,1024]{1,0:T(8,128)}), (f32[256,768]{1,0:T(8,128)}, f32[256,256]{1,0:T(8,128)}, f32[256,1024]{1,0:T(8,128)}, ...) | async-done | bytes 3145744 | tf_op jit(solution)/shard_map/psum | solution.py:258
  263.3 0.0 copy-start.1
  263.3 1.3 multiply_bitcast_fusion
  264.6 0.0 copy-start
  264.6 1.3 copy.16
  265.9 0.0 copy-done.1
  265.9 0.7 broadcast_multiply_fusion.2
  266.7 2.1 broadcast_multiply_fusion.1
  268.7 0.0 copy-done
  268.7 1.0 broadcast_multiply_fusion
  269.8 0.0 all-to-all-done.1
  269.8 1.1 copy.15
Async XLA Ops:
  7.2 256.1 %all-reduce.3.cloned.1.call-start = ((), (), s32[]{:S(2)}) async-start(), calls=%async_computation.2 | async-start | bytes 6291456 | tf_op jit(solution)/shard_map/psum | solution.py:258
  111.9 3.2 %copy-start.2 = (f32[2,256]{1,0:T(2,128)S(1)}, f32[2,256]{1,0:T(2,128)}, u32[]{:S(2)}) copy-start(f32[2,256]{1,0:T(2,128)} %get-tuple-element.17) | copy-start | bytes 6148
  111.9 157.8 %all-to-all-start.1 = ((bf16[32,4,16,256]{3,2,1,0:T(8,128)(2,1)}), bf16[32,4,16,256]{3,2,1,0:T(8,128)(2,1)S(1)}, u32[]{:S(2)}, u32[]{:S(2)}) async-start(bf16[32,4,16,256]{3,2,1,0:T(8,128)(2,1)} %get-tuple-element.12), calls=%async_computation.1 | async-start | bytes 2097152 | tf_op jit(solution)/shard_map/all_to_all | solution.py:249
  263.3 2.7 copy-start.1
  264.6 4.1 %copy-start = (f32[256,1024]{1,0:T(8,128)S(1)}, f32[256,1024]{1,0:T(8,128)}, u32[]{:S(2)}) copy-start(f32[256,1024]{1,0:T(8,128)} %get-tuple-element.26) | copy-start | bytes 3145732
Sparse Core Ops, SparseCore 0:
  112.1 151.1 all-reduce.2
where the time goes:
time: 280 us; the launch traced here: 278 us
  blocking collectives  113 us (40%)
  waiting for transfers between devices  90.4 us (32%)
  Pallas kernels  46.9 us (17%)
  between operations  14.1 us (5%)
  other arithmetic  5.94 us (2%)
  local copies, waits for them, and re-layouts  4.15 us (1%)
  starting transfers between devices  3.19 us (1%)
    psum x1, waiting for transfers between devices, shards(): totals = lax.psum(tuple(sums), ('ha', 'wa'))  90.4 us
    psum x1, blocking collectives, shards(): totals = lax.psum(tuple(sums), ('ha', 'wa'))  57.2 us
    all_to_all x1, blocking collectives, exchange(): return lax.all_to_all(x, ('ha', 'wa'), 0, 0, tiled=True)  55.8 us
    pallas_call x1, Pallas kernels, local_call(): pl.pallas_call(local_kernel, grid=(chunks,), in_specs=[pl.BlockSpec((peer...  46.9 us
  transfers between devices with their start and end apart: 2, of which 1 were waited for; matrix products, arithmetic and copies ran while one was open for 3% of the time, Pallas kernels for 0%

commit v1 on v0

--- a/solution.py
+++ b/solution.py
@@ -216,6 +216,180 @@
     )(x, wqkv, wout, wup, wdown, gains)
 
 
+def reduce_kernel(
+    rows_dev, cols_dev, factor,
+    s_qkv, s_out, s_up, s_down, s_gain,
+    o_qkv, o_out, o_up, o_down, o_gain,
+    work, send, recv, total, gsend, grecv, gwide, send_sem, recv_sem,
+):
+    mesh_id = pl.DeviceIdType.MESH
+    bits = rows_dev.bit_length() - 1
+    half_rows = work.shape[1]
+    ha, wa = lax.axis_index("ha"), lax.axis_index("wa")
+    side = [(ha // (1 << b)) % 2 for b in range(bits)]
+    partner = [(ha + (1 - 2 * side[b]) * (1 << b), wa) for b in range(bits)]
+    across = [(ha, lax.rem(wa + i, cols_dev)) for i in range(1, cols_dev)]
+
+    barrier = pltpu.get_barrier_semaphore()
+    for device in partner + across:
+        pl.semaphore_signal(barrier, inc=1, device_id=device, device_id_type=mesh_id)
+    pl.semaphore_wait(barrier, len(partner) + len(across))
+
+    count = [0]
+    copies = []
+
+    def push(src, dst, device):
+        k = count[0]
+        count[0] += 1
+        copy = pltpu.make_async_remote_copy(
+            src_ref=src, dst_ref=dst, send_sem=send_sem.at[k], recv_sem=recv_sem.at[k],
+            device_id=device, device_id_type=mesh_id,
+        )
+        copy.start()
+        copies.append(copy)
+        return copy
+
+    places = []
+    block = s_qkv.shape[0]
+    per_half = half_rows // block
+    for src, dst, flip in ((s_qkv, o_qkv, 0), (s_out, o_out, 0), (s_up, o_up, 0), (s_down, o_down, 1)):
+        for start in range(0, src.shape[1], LANES):
+            places.append((src, dst, flip, start))
+    used = -(-len(places) // 2)
+    for n, (src, _, _, start) in enumerate(places):
+        row = n % used * block
+        work[n // used, row : row + block, :] = src[:, start : start + LANES]
+    if used < per_half:
+        work[:, used * block :, :] = jnp.zeros((2, half_rows - used * block, LANES), F32)
+
+    def span(start, size):
+        return pl.ds(pl.multiple_of(start, ROWS), size)
+
+    orders = [[0] + list(range(1, bits)), [0] + list(range(bits - 1, 0, -1))]
+    start = [0, 0]
+    size = half_rows
+    offset = 0
+    pending = [None, None]
+    gsend[0] = jnp.zeros(gsend.shape[1:], F32)
+    gsend[0, 0:2, :] = s_gain[...]
+    gpending = None
+
+    def absorb(h):
+        if pending[h] is None:
+            return
+        copy, at, n = pending[h]
+        copy.wait_recv()
+        place = span(start[h], n)
+        work[h, place, :] = work[h, place, :] + recv[h, at : at + n, :].astype(F32)
+
+    for step in range(bits):
+        half = size // 2
+        for h in range(2):
+            absorb(h)
+            b = orders[h][step]
+            send[h, offset : offset + half, :] = work[h, span(start[h] + (1 - side[b]) * half, half), :].astype(BF)
+            copy = push(
+                send.at[h, pl.ds(offset, half), :], recv.at[h, pl.ds(offset, half), :], partner[b]
+            )
+            start[h] = start[h] + side[b] * half
+            pending[h] = (copy, offset, half)
+        if step > 0:
+            gpending.wait_recv()
+            gsend[step] = gsend[step - 1] + grecv[step - 1]
+        gpending = push(gsend.at[step], grecv.at[step], partner[step])
+        offset += half
+        size = half
+
+    shard = size // cols_dev
+    arrivals = [[], []]
+    for h in range(2):
+        absorb(h)
+        for i in range(1, cols_dev):
+            peer = across[i - 1]
+            at = offset + (i - 1) * shard
+            send[h, at : at + shard, :] = work[h, span(start[h] + peer[1] * shard, shard), :].astype(BF)
+            arrivals[h].append(
+                push(send.at[h, pl.ds(at, shard), :], recv.at[h, pl.ds(at, shard), :], peer)
+            )
+    gpending.wait_recv()
+    gwide[wa] = gsend[bits - 1] + grecv[bits - 1]
+    garrivals = [push(gwide.at[wa], gwide.at[wa], peer) for peer in across]
+
+    gathers = [[], []]
+    for h in range(2):
+        mine = span(start[h] + wa * shard, shard)
+        value = work[h, mine, :]
+        for i in range(1, cols_dev):
+            arrivals[h][i - 1].wait_recv()
+            at = offset + (i - 1) * shard
+            value = value + recv[h, at : at + shard, :].astype(F32)
+        total[h, mine, :] = value.astype(BF)
+        for peer in across:
+            gathers[h].append(push(total.at[h, mine, :], total.at[h, mine, :], peer))
+    for step in reversed(range(bits)):
+        for h in range(2):
+            for copy in gathers[h]:
+                copy.wait_recv()
+            b = orders[h][step]
+            held = total.at[h, span(start[h], size), :]
+            gathers[h] = [push(held, held, partner[b])]
+            start[h] = start[h] - side[b] * size
+        size = size * 2
+    for copy in garrivals:
+        copy.wait_recv()
+    gain = gwide[0]
+    for i in range(1, cols_dev):
+        gain = gain + gwide[i]
+    o_gain[...] = gain[0:2, :] * factor
+    for h in range(2):
+        for copy in gathers[h]:
+            copy.wait_recv()
+    for n, (_, dst, flip, at) in enumerate(places):
+        row = n % used * block
+        value = total[n // used, row : row + block, :].astype(F32) * factor
+        if flip:
+            dst[at : at + LANES, :] = value.T
+        else:
+            dst[:, at : at + LANES] = value
+    for copy in copies:
+        copy.wait_send()
+
+
+def reduce_scratch(rows_dev, cols_dev, elements, channels):
+    bits = rows_dev.bit_length() - 1
+    unit = ROWS * rows_dev * cols_dev
+    half_rows = -(-elements // (2 * LANES * unit)) * unit
+    moved = half_rows - half_rows // rows_dev + half_rows // rows_dev // cols_dev * (cols_dev - 1)
+    number = 5 * (cols_dev - 1) + 5 * bits
+    return [
+        pltpu.VMEM((2, half_rows, LANES), F32),
+        pltpu.VMEM((2, moved, LANES), BF),
+        pltpu.VMEM((2, moved, LANES), BF),
+        pltpu.VMEM((2, half_rows, LANES), BF),
+        pltpu.VMEM((bits, 8, channels), F32),
+        pltpu.VMEM((bits, 8, channels), F32),
+        pltpu.VMEM((cols_dev, 8, channels), F32),
+        pltpu.SemaphoreType.DMA((number,)),
+        pltpu.SemaphoreType.DMA((number,)),
+    ]
+
+
+def reduce_call(rows_dev, cols_dev, factor, sums):
+    shapes = [s.shape for s in sums]
+    shapes[3] = shapes[3][::-1]
+    elements = sum(math.prod(s) for s in shapes[:4])
+    return pl.pallas_call(
+        functools.partial(reduce_kernel, rows_dev, cols_dev, factor),
+        in_specs=[pl.BlockSpec(memory_space=pltpu.VMEM)] * 5,
+        out_specs=[pl.BlockSpec(memory_space=pltpu.VMEM)] * 5,
+        out_shape=[jax.ShapeDtypeStruct(s, F32) for s in shapes],
+        scratch_shapes=reduce_scratch(rows_dev, cols_dev, elements, shapes[0][0]),
+        compiler_params=pltpu.CompilerParams(
+            collective_id=0, has_side_effects=True, vmem_limit_bytes=40 << 20
+        ),
+    )(*sums)
+
+
 def layout(rows_dev, cols_dev, tile_rows, tile_cols):
     stride_h = tile_rows * rows_dev // GRID
     stride_w = tile_cols * cols_dev // GRID
@@ -255,17 +429,9 @@
 
     arrived = exchange(jnp.stack([pack(features), pack(cotangent)], axis=2))
     done, *sums = local_call(arrived, qkv_weight, out_weight, up_weight, down_weight, norm_gains)
-    totals = lax.psum(tuple(sums), ("ha", "wa"))
-    grad_input = unpack(exchange(done))
     factor = 1.0 / float(images * tile_rows * tile_cols * rows_dev * cols_dev) ** 0.5
-    return (
-        grad_input,
-        totals[0] * factor,
-        totals[1] * factor,
-        totals[2] * factor,
-        totals[3].T * factor,
-        totals[4] * factor,
-    )
+    totals = reduce_call(rows_dev, cols_dev, factor, sums)
+    return (unpack(exchange(done)), *totals)
 
 
 def solution(mesh):

time: 280 us -> 164 us (0.59)
  waiting for transfers between devices: 90.4 us -> 0.01 us
  blocking collectives: 113 us -> 55.8 us
  Pallas kernels: 46.9 us -> 91.4 us
  between operations: 14.1 us -> 0.72 us
  local copies, waits for them, and re-layouts: 4.15 us -> 12.4 us
  other arithmetic: 5.94 us -> 0.18 us
    psum x1 -> x0, waiting for transfers between devices: 90.4 us -> none  [shards(): totals = lax.psum(tuple(sums), ('ha', 'wa'))]
    psum x1 -> x0, blocking collectives: 57.2 us -> none  [shards(): totals = lax.psum(tuple(sums), ('ha', 'wa'))]
    pallas_call x0 -> x1, Pallas kernels: none -> 44.5 us  [reduce_call(): pl.pallas_call(functools.partial(reduce_kernel, rows_dev, cols_dev, facto...]
    unnamed x7 -> x19, local copies, waits for them, and re-layouts: 1.32 us -> 8.29 us
    mul x5 -> x0, other arithmetic: 5.76 us -> none  [the longest x1 2.06 us: shards(): totals[0] * factor]
  transfers between devices with their start and end apart: 2 -> 1, of which waited for: 1 -> 0; matrix products, arithmetic and copies ran while one was open for 3% -> 0% of each run, Pallas kernels for 0% -> 27%
where the time goes in v1:
time: 164 us
  Pallas kernels  91.4 us (56%)
  blocking collectives  55.8 us (34%)
  local copies, waits for them, and re-layouts  12.4 us (8%)
  starting transfers between devices  3.28 us (2%)
    all_to_all x1, blocking collectives, exchange(): return lax.all_to_all(x, ('ha', 'wa'), 0, 0, tiled=True)  55.8 us
    pallas_call x1, Pallas kernels, local_call(): pl.pallas_call(local_kernel, grid=(chunks,), in_specs=[pl.BlockSpec((peer...  46.9 us
    pallas_call x1, Pallas kernels, reduce_call(): pl.pallas_call(functools.partial(reduce_kernel, rows_dev, cols_dev, facto...  44.5 us
    unnamed x19, local copies, waits for them, and re-layouts  8.29 us
  transfers between devices with their start and end apart: 1, of which 0 were waited for; matrix products, arithmetic and copies ran while one was open for 0% of the time, Pallas kernels for 27%

profile of v1, /device:TPU:1, one launch (start us, length us, event | category | flops | bytes accessed | tf_op | source)
XLA Modules:
  0.0 163.8 jit_solution(8175213292306403740)
XLA Ops:
  0.6 1.7 %copy_bitcast_fusion = (bf16[32,4,1,16,256]{4,3,2,1,0:T(8,128)(2,1)S(1)}, bf16[32,4,1,16,256]{4,3,2,1,0:T(8,128)(2,1)S(1)}) fusion(bf16[32,2,1,4,8,256]{5,4,3,1,0,2:T(8,128)(2,1)} %bitcast.15, bf16[32,2,1,4,8,256]{5,4,3,1,0,2:T(8,128)(2,1)} %bitcast.16), kind=kLoop, calls=%fused_computation.1 | loop fusion | bytes 4194304 | tf_op jit(solution)/shard_map/stack;reshape | solution.py:430
  2.4 0.2 pad_maximum_fusion
  2.6 55.8 %all_to_all.10.x_ref = bf16[32,4,2,16,256]{4,3,2,1,0:T(8,128)(2,1)} all-to-all(bf16[32,4,2,16,256]{4,3,2,1,0:T(8,128)(2,1)S(1)} %pad_maximum_fusion), channel_id=1, replica_groups=mesh['ha'=8,'wa'=4] {'ha','wa'}, dimensions={0} | all-to-all | bytes 4194304 | tf_op jit(solution)/shard_map/all_to_all | solution.py:423
  58.4 46.9 %shard_map.118 = (bf16[32,4,16,256]{3,2,1,0:T(8,128)(2,1)}, f32[256,768]{1,0:T(8,128)}, f32[256,256]{1,0:T(8,128)}, f32[256,1024]{1,0:T(8,128)}, f32[256,1024]{1,0:T(8,128)}, /*index=5*/f32[2,256]{1,0:T(2,128)}) custom-call(bf16[32,4,2,16,256]{4,3,2,1,0:T(8,128)(2,1)} %all_to_all.10.x_ref, bf16[256,768]{1,0:T(8,128)(2,1)} %wqkv.1, bf16[256,256]{1,0:T(8,128)(2,1)} %wout.1, ...), custom_call_target="tpu_custom_call" | custom-call | tf_op jit(solution)/shard_map/pallas_call | solution.py:205
  105.3 0.0 copy-start
  105.3 0.0 copy-start.6
  105.4 3.3 %all-to-all-start.1 = ((bf16[32,4,16,256]{3,2,1,0:T(8,128)(2,1)}), bf16[32,4,16,256]{3,2,1,0:T(8,128)(2,1)}, u32[]{:S(2)}, u32[]{:S(2)}) async-start(bf16[32,4,16,256]{3,2,1,0:T(8,128)(2,1)} %get-tuple-element.17), calls=%async_computation.1 | async-start | bytes 2097152 | tf_op jit(solution)/shard_map/all_to_all | solution.py:423
  108.6 0.0 copy-done
  108.6 0.0 copy-done.6
  108.7 0.0 copy-start.1
  108.7 1.2 copy-done.1
  109.9 0.0 copy-start.4
  109.9 1.1 copy-done.4
  111.0 0.0 copy-start.5
  111.0 0.9 copy-done.5
  112.0 44.5 %shard_map.119 = (f32[256,768]{1,0:T(8,128)S(1)}, f32[256,256]{1,0:T(8,128)S(1)}, f32[256,1024]{1,0:T(8,128)S(1)}, f32[1024,256]{1,0:T(8,128)S(1)}, f32[2,256]{1,0:T(2,128)S(1)}) custom-call(f32[256,768]{1,0:T(8,128)S(1)} %copy-done.4, f32[256,256]{1,0:T(8,128)S(1)} %copy-done.5, f32[256,1024]{1,0:T(8,128)S(1)} %copy-done, f32[256,1024]{1,0:T(8,128)S(1)} %copy-done.1, ...), custom_call_target="tpu_custom_call" | custom-call | tf_op jit(solution)/shard_map/pallas_call | solution.py:381
  156.4 0.0 copy-start.2
  156.5 0.9 copy-done.2
  157.3 0.0 copy-start.3
  157.3 0.0 all-to-all-done.1
  157.3 2.4 %copy.15 = bf16[32,2,1,4,8,256]{5,4,3,1,0,2:T(8,128)(2,1)} copy(bf16[32,2,1,4,8,256]{5,4,1,3,0,2:T(8,128)(2,1)} %bitcast.7) | data formatting | bytes 2097152 | tf_op jit(solution)/shard_map/transpose | solution.py:419
  159.7 0.0 copy-done.3
  159.7 0.9 copy.23
  160.6 0.7 copy.24
  161.3 1.0 copy.25
  162.3 1.0 copy.26
  163.3 0.6 copy.27
Async XLA Ops:
  105.3 3.3 %copy-start = (f32[256,1024]{1,0:T(8,128)S(1)}, f32[256,1024]{1,0:T(8,128)}, u32[]{:S(2)}) copy-start(f32[256,1024]{1,0:T(8,128)} %get-tuple-element.20.s_up) | copy-start | bytes 3145732
  105.3 3.3 %copy-start.6 = (f32[2,256]{1,0:T(2,128)S(1)}, f32[2,256]{1,0:T(2,128)}, u32[]{:S(2)}) copy-start(f32[2,256]{1,0:T(2,128)} %get-tuple-element.22.s_gain) | copy-start | bytes 6148
  105.4 52.0 %all-to-all-start.1 = ((bf16[32,4,16,256]{3,2,1,0:T(8,128)(2,1)}), bf16[32,4,16,256]{3,2,1,0:T(8,128)(2,1)}, u32[]{:S(2)}, u32[]{:S(2)}) async-start(bf16[32,4,16,256]{3,2,1,0:T(8,128)(2,1)} %get-tuple-element.17), calls=%async_computation.1 | async-start | bytes 2097152 | tf_op jit(solution)/shard_map/all_to_all | solution.py:423
  108.7 1.2 copy-start.1
  109.9 1.1 copy-start.4
  111.0 0.9 copy-start.5
  156.4 0.9 copy-start.2
  157.3 2.4 %copy-start.3 = (f32[256,768]{1,0:T(8,128)S(1)}, f32[256,768]{1,0:T(8,128)}, u32[]{:S(2)}) copy-start(f32[256,768]{1,0:T(8,128)} %copy-done.2) | copy-start | bytes 2359300

commit v2 on v1

--- a/solution.py
+++ b/solution.py
@@ -161,24 +161,85 @@
     store_out(jnp.concatenate([reg[half] for half in range(halves)], axis=1).astype(BF))
 
 
-def local_kernel(x_ref, wqkv, wout, wup, wdown, gains, o_ref, *rest):
-    sums, scratch = rest[:5], rest[5:]
-    peers, _, _, piece, channels = x_ref.shape
+def fused_kernel(
+    rows_dev, cols_dev, classes, factor,
+    x_ref, wqkv, wout, wup, wdown, gains,
+    o_ref, o_qkv, o_out, o_up, o_down, o_gain, *scratch,
+):
+    arrived, finished, in_send, in_recv, out_send, out_recv = scratch[:6]
+    sums, work, reduce_work = scratch[6:11], scratch[11:16], scratch[16:]
+    chunks, peers, _, piece, channels = x_ref.shape
     rows = peers * piece
-
-    @pl.when(pl.program_id(0) == 0)
-    def _():
-        for ref in sums:
-            ref[...] = jnp.zeros_like(ref)
-
-    def store(value):
-        o_ref[:, 0] = value.reshape(peers, piece, channels)
-
-    chunk_work(
-        lambda: x_ref[:, 0, 0].reshape(rows, channels),
-        lambda: x_ref[:, 0, 1].reshape(rows, channels),
-        store, None, wqkv, wout, wup, wdown, gains, *sums, *scratch,
+    mesh_id = pl.DeviceIdType.MESH
+    ha, wa = lax.axis_index("ha"), lax.axis_index("wa")
+    kind = ha % classes
+    me = ha // classes * cols_dev + wa
+
+    def device_of(i):
+        e = lax.rem(me + i, peers)
+        return e, (e // cols_dev * classes + kind, lax.rem(e, cols_dev))
+
+    barrier = pltpu.get_barrier_semaphore()
+
+    @pl.loop(1, peers)
+    def _(i):
+        pl.semaphore_signal(barrier, inc=1, device_id=device_of(i)[1], device_id_type=mesh_id)
+
+    extra = classes.bit_length() - 1
+    for b in range(extra):
+        other = ha + (1 - 2 * ((ha // (1 << b)) % 2)) * (1 << b)
+        pl.semaphore_signal(barrier, inc=1, device_id=(other, wa), device_id_type=mesh_id)
+    pl.semaphore_wait(barrier, peers - 1 + extra)
+
+    def scatter(src, dst, c, send_sem, recv_sem):
+        pltpu.make_async_copy(src.at[c, me], dst.at[c, me], recv_sem.at[c]).start()
+
+        @pl.loop(1, peers)
+        def _(i):
+            e, device = device_of(i)
+            pltpu.make_async_remote_copy(
+                src_ref=src.at[c, e], dst_ref=dst.at[c, me],
+                send_sem=send_sem.at[c], recv_sem=recv_sem.at[c],
+                device_id=device, device_id_type=mesh_id,
+            ).start()
+
+    def all_of(ref, c, sem):
+        pltpu.make_async_copy(ref.at[c], ref.at[c], sem.at[c]).wait()
+
+    def all_sent(ref, c, sem):
+        part = ref.at[c, pl.ds(0, peers - 1)]
+        pltpu.make_async_copy(part, part, sem.at[c]).wait()
+
+    @pl.loop(0, chunks)
+    def _(c):
+        scatter(x_ref, arrived, c, in_send, in_recv)
+
+    for ref in sums:
+        ref[...] = jnp.zeros_like(ref)
+
+    @pl.loop(0, chunks)
+    def _(c):
+        all_of(arrived, c, in_recv)
+
+        def store(value):
+            finished[c] = value.reshape(peers, piece, channels)
+
+        chunk_work(
+            lambda: arrived[c, :, 0].reshape(rows, channels),
+            lambda: arrived[c, :, 1].reshape(rows, channels),
+            store, None, wqkv, wout, wup, wdown, gains, *sums, *work,
+        )
+        scatter(finished, o_ref, c, out_send, out_recv)
+
+    reduce_steps(
+        rows_dev, cols_dev, factor, *sums, o_qkv, o_out, o_up, o_down, o_gain, *reduce_work
     )
+
+    @pl.loop(0, chunks)
+    def _(c):
+        all_of(o_ref, c, out_recv)
+        all_sent(finished, c, out_send)
+        all_sent(x_ref, c, in_send)
 
 
 def scratch_of(rows, channels):
@@ -194,29 +255,7 @@
     ]
 
 
-def local_call(x, wqkv, wout, wup, wdown, gains):
-    peers, chunks, _, piece, channels = x.shape
-    hidden = wup.shape[1]
-
-    def whole(shape):
-        return pl.BlockSpec(shape, lambda c: (0,) * len(shape))
-
-    sums = [(channels, 3 * channels), (channels, channels), (channels, hidden), (channels, hidden), (2, channels)]
-    return pl.pallas_call(
-        local_kernel,
-        grid=(chunks,),
-        in_specs=[pl.BlockSpec((peers, 1, 2, piece, channels), lambda c: (0, c, 0, 0, 0))]
-        + [whole(a.shape) for a in (wqkv, wout, wup, wdown, gains)],
-        out_specs=[pl.BlockSpec((peers, 1, piece, channels), lambda c: (0, c, 0, 0))]
-        + [whole(s) for s in sums],
-        out_shape=[jax.ShapeDtypeStruct((peers, chunks, piece, channels), BF)]
-        + [jax.ShapeDtypeStruct(s, F32) for s in sums],
-        scratch_shapes=scratch_of(peers * piece, channels),
-        compiler_params=pltpu.CompilerParams(vmem_limit_bytes=56 << 20),
-    )(x, wqkv, wout, wup, wdown, gains)
-
-
-def reduce_kernel(
+def reduce_steps(
     rows_dev, cols_dev, factor,
     s_qkv, s_out, s_up, s_down, s_gain,
     o_qkv, o_out, o_up, o_down, o_gain,
@@ -229,11 +268,6 @@
     side = [(ha // (1 << b)) % 2 for b in range(bits)]
     partner = [(ha + (1 - 2 * side[b]) * (1 << b), wa) for b in range(bits)]
     across = [(ha, lax.rem(wa + i, cols_dev)) for i in range(1, cols_dev)]
-
-    barrier = pltpu.get_barrier_semaphore()
-    for device in partner + across:
-        pl.semaphore_signal(barrier, inc=1, device_id=device, device_id_type=mesh_id)
-    pl.semaphore_wait(barrier, len(partner) + len(across))
 
     count = [0]
     copies = []
@@ -374,20 +408,32 @@
     ]
 
 
-def reduce_call(rows_dev, cols_dev, factor, sums):
-    shapes = [s.shape for s in sums]
-    shapes[3] = shapes[3][::-1]
+def fused_call(rows_dev, cols_dev, classes, factor, x, *weights):
+    chunks, peers, _, piece, channels = x.shape
+    hidden = weights[2].shape[1]
+    shapes = [(channels, 3 * channels), (channels, channels), (channels, hidden), (hidden, channels), (2, channels)]
+    held = shapes[:3] + [(channels, hidden), (2, channels)]
     elements = sum(math.prod(s) for s in shapes[:4])
+    vmem = pl.BlockSpec(memory_space=pltpu.VMEM)
+    anywhere = pl.BlockSpec(memory_space=pl.ANY)
     return pl.pallas_call(
-        functools.partial(reduce_kernel, rows_dev, cols_dev, factor),
-        in_specs=[pl.BlockSpec(memory_space=pltpu.VMEM)] * 5,
-        out_specs=[pl.BlockSpec(memory_space=pltpu.VMEM)] * 5,
-        out_shape=[jax.ShapeDtypeStruct(s, F32) for s in shapes],
-        scratch_shapes=reduce_scratch(rows_dev, cols_dev, elements, shapes[0][0]),
+        functools.partial(fused_kernel, rows_dev, cols_dev, classes, factor),
+        in_specs=[anywhere] + [vmem] * 5,
+        out_specs=[anywhere] + [vmem] * 5,
+        out_shape=[jax.ShapeDtypeStruct((chunks, peers, piece, channels), BF)]
+        + [jax.ShapeDtypeStruct(s, F32) for s in shapes],
+        scratch_shapes=[
+            pltpu.VMEM((chunks, peers, 2, piece, channels), BF),
+            pltpu.VMEM((chunks, peers, piece, channels), BF),
+        ]
+        + [pltpu.SemaphoreType.DMA((chunks,))] * 4
+        + [pltpu.VMEM(s, F32) for s in held]
+        + scratch_of(peers * piece, channels)
+        + reduce_scratch(rows_dev, cols_dev, elements, channels),
         compiler_params=pltpu.CompilerParams(
-            collective_id=0, has_side_effects=True, vmem_limit_bytes=40 << 20
+            collective_id=0, has_side_effects=True, vmem_limit_bytes=56 << 20
         ),
-    )(*sums)
+    )(x, *weights)
 
 
 def layout(rows_dev, cols_dev, tile_rows, tile_cols):
@@ -411,27 +457,20 @@
     split = (tile_rows, inner, cuts, chunks, per_chunk, channels)
 
     def pack(tile):
-        cut = jnp.transpose(tile.reshape(split), (0, 2, 3, 1, 4, 5))
-        return cut.reshape(peers, chunks, ROWS, channels)
+        cut = jnp.transpose(tile.reshape(split), (3, 0, 2, 1, 4, 5))
+        return cut.reshape(chunks, peers, ROWS, channels)
 
     def unpack(packed):
-        cut = packed.reshape(tile_rows, cuts, chunks, inner, per_chunk, channels)
-        return jnp.transpose(cut, (0, 3, 1, 2, 4, 5)).reshape(images, tile_rows, tile_cols, channels)
-
-    def exchange(x):
-        if classes == 1:
-            return lax.all_to_all(x, ("ha", "wa"), 0, 0, tiled=True)
-        everyone = [
-            [(h * classes + c) * cols_dev + w for h in range(rows_dev // classes) for w in range(cols_dev)]
-            for c in range(classes)
-        ]
-        return lax.all_to_all(x, ("ha", "wa"), 0, 0, tiled=True, axis_index_groups=everyone)
-
-    arrived = exchange(jnp.stack([pack(features), pack(cotangent)], axis=2))
-    done, *sums = local_call(arrived, qkv_weight, out_weight, up_weight, down_weight, norm_gains)
+        cut = packed.reshape(chunks, tile_rows, cuts, inner, per_chunk, channels)
+        return jnp.transpose(cut, (1, 3, 2, 0, 4, 5)).reshape(images, tile_rows, tile_cols, channels)
+
+    packed = jnp.stack([pack(features), pack(cotangent)], axis=2)
     factor = 1.0 / float(images * tile_rows * tile_cols * rows_dev * cols_dev) ** 0.5
-    totals = reduce_call(rows_dev, cols_dev, factor, sums)
-    return (unpack(exchange(done)), *totals)
+    done, *totals = fused_call(
+        rows_dev, cols_dev, classes, factor, packed,
+        qkv_weight, out_weight, up_weight, down_weight, norm_gains,
+    )
+    return (unpack(done), *totals)
 
 
 def solution(mesh):

time: 164 us -> 127 us (0.77)
  blocking collectives: 55.8 us -> 0 us
  Pallas kernels: 91.4 us -> 116 us
  local copies, waits for them, and re-layouts: 12.4 us -> 8.33 us
  starting transfers between devices: 3.28 us -> 0 us
    all_to_all x1 -> x0, blocking collectives: 55.8 us -> none  [exchange(): return lax.all_to_all(x, ('ha', 'wa'), 0, 0, tiled=True)]
    pallas_call x2 -> x1, Pallas kernels: 91.4 us -> 116 us  [fused_call(): pl.pallas_call(functools.partial(fused_kernel, rows_dev, cols_dev, classe...]
    unnamed x19 -> x15, local copies, waits for them, and re-layouts: 8.29 us -> 4.12 us
    all_to_all x1 -> x0, starting transfers between devices: 3.28 us -> none  [exchange(): return lax.all_to_all(x, ('ha', 'wa'), 0, 0, tiled=True)]
  transfers between devices with their start and end apart: 1 -> 0, of which waited for: 0 -> 0; matrix products, arithmetic and copies ran while one was open for 0% -> 0% of each run, Pallas kernels for 27% -> 0%
where the time goes in v2:
time: 127 us
  Pallas kernels  116 us (91%)
  local copies, waits for them, and re-layouts  8.33 us (7%)
  other arithmetic  1.54 us (1%)
    pallas_call x1, Pallas kernels, fused_call(): pl.pallas_call(functools.partial(fused_kernel, rows_dev, cols_dev, classe...  116 us
    unnamed x15, local copies, waits for them, and re-layouts  4.12 us

profile of v2, /device:TPU:1, one launch (start us, length us, event | category | flops | bytes accessed | tf_op | source)
XLA Modules:
  0.0 126.6 jit_solution(16652822811028145664)
XLA Ops:
  0.6 1.7 %copy_bitcast_fusion = (bf16[4,32,1,16,256]{4,3,2,1,0:T(8,128)(2,1)S(1)}, bf16[4,32,1,16,256]{4,3,2,1,0:T(8,128)(2,1)S(1)}) fusion(bf16[32,2,1,4,8,256]{5,4,3,1,0,2:T(8,128)(2,1)} %bitcast.16, bf16[32,2,1,4,8,256]{5,4,3,1,0,2:T(8,128)(2,1)} %bitcast.17), kind=kLoop, calls=%fused_computation.1 | loop fusion | bytes 4194304 | tf_op jit(solution)/shard_map/stack;reshape | solution.py:467
  2.4 1.5 %pad_maximum_fusion.x_ref = bf16[4,32,2,16,256]{4,3,2,1,0:T(8,128)(2,1)} fusion(bf16[4,32,1,16,256]{4,3,2,1,0:T(8,128)(2,1)S(1)} %get-tuple-element.18, bf16[4,32,1,16,256]{4,3,2,1,0:T(8,128)(2,1)S(1)} %get-tuple-element.19), kind=kLoop, calls=%fused_computation | loop fusion | flops 1048576 | bytes 4194304 | tf_op jit(solution)/shard_map/stack | solution.py:467
  3.9 116.0 %shard_map.118 = (bf16[4,32,16,256]{3,2,1,0:T(8,128)(2,1)}, f32[256,768]{1,0:T(8,128)}, f32[256,256]{1,0:T(8,128)}, f32[256,1024]{1,0:T(8,128)}, f32[1024,256]{1,0:T(8,128)}, /*index=5*/f32[2,256]{1,0:T(2,128)}) custom-call(bf16[4,32,2,16,256]{4,3,2,1,0:T(8,128)(2,1)} %pad_maximum_fusion.x_ref, bf16[256,768]{1,0:T(8,128)(2,1)} %wqkv.1, ...), custom_call_target="tpu_custom_call" | custom-call | tf_op jit(solution)/shard_map/pallas_call | solution.py:419
  120.0 0.0 copy-start.2
  120.0 0.0 copy-start.3
  120.0 0.0 copy-start.1
  120.0 2.5 %copy.15 = bf16[32,2,1,4,8,256]{5,4,3,1,0,2:T(8,128)(2,1)} copy(bf16[32,2,1,4,8,256]{5,4,1,0,3,2:T(8,128)(2,1)} %bitcast.15) | data formatting | bytes 2097152 | tf_op jit(solution)/shard_map/transpose | solution.py:465
  122.5 0.0 copy-done.2
  122.5 0.0 copy-start
  122.5 0.9 copy.23
  123.4 0.0 copy-done.3
  123.4 0.7 copy.24
  124.1 0.0 copy-done.1
  124.1 0.0 copy-start.4
  124.1 1.0 copy.25
  125.0 0.0 copy-done
  125.0 1.0 copy.26
  126.0 0.0 copy-done.4
  126.0 0.6 copy.27
Async XLA Ops:
  120.0 2.5 %copy-start.2 = (f32[256,768]{1,0:T(8,128)S(1)}, f32[256,768]{1,0:T(8,128)}, u32[]{:S(2)}) copy-start(f32[256,768]{1,0:T(8,128)} %get-tuple-element.27) | copy-start | bytes 2359300
  120.0 3.4 %copy-start.3 = (f32[256,256]{1,0:T(8,128)S(1)}, f32[256,256]{1,0:T(8,128)}, u32[]{:S(2)}) copy-start(f32[256,256]{1,0:T(8,128)} %get-tuple-element.28) | copy-start | bytes 786436
  120.0 4.1 %copy-start.1 = (f32[256,1024]{1,0:T(8,128)S(1)}, f32[256,1024]{1,0:T(8,128)}, u32[]{:S(2)}) copy-start(f32[256,1024]{1,0:T(8,128)} %get-tuple-element.29) | copy-start | bytes 3145732
  122.5 2.6 %copy-start = (f32[1024,256]{1,0:T(8,128)S(1)}, f32[1024,256]{1,0:T(8,128)}, u32[]{:S(2)}) copy-start(f32[1024,256]{1,0:T(8,128)} %get-tuple-element.30) | copy-start | bytes 3145732
  124.1 1.9 %copy-start.4 = (f32[2,256]{1,0:T(2,128)S(1)}, f32[2,256]{1,0:T(2,128)}, u32[]{:S(2)}) copy-start(f32[2,256]{1,0:T(2,128)} %get-tuple-element.31) | copy-start | bytes 6148

commit v3 on v2

--- a/solution.py
+++ b/solution.py
@@ -176,7 +176,8 @@
     me = ha // classes * cols_dev + wa
 
     def device_of(i):
-        e = lax.rem(me + i, peers)
+        tall = peers // cols_dev
+        e = lax.rem(me // cols_dev + lax.rem(i, tall), tall) * cols_dev + lax.rem(wa + i // tall, cols_dev)
         return e, (e // cols_dev * classes + kind, lax.rem(e, cols_dev))
 
     barrier = pltpu.get_barrier_semaphore()
@@ -210,7 +211,9 @@
         part = ref.at[c, pl.ds(0, peers - 1)]
         pltpu.make_async_copy(part, part, sem.at[c]).wait()
 
-    @pl.loop(0, chunks)
+    ahead = 2
+
+    @pl.loop(0, ahead)
     def _(c):
         scatter(x_ref, arrived, c, in_send, in_recv)
 
@@ -220,6 +223,10 @@
     @pl.loop(0, chunks)
     def _(c):
         all_of(arrived, c, in_recv)
+
+        @pl.when(c + ahead < chunks)
+        def _():
+            scatter(x_ref, arrived, c + ahead, in_send, in_recv)
 
         def store(value):
             finished[c] = value.reshape(peers, piece, channels)

time: 127 us -> 124 us (0.976)
  Pallas kernels: 116 us -> 113 us
    pallas_call x1, Pallas kernels: 116 us -> 113 us  [fused_call(): pl.pallas_call(functools.partial(fused_kernel, rows_dev, cols_dev, classe...]
where the time goes in v3:
time: 124 us
  Pallas kernels  113 us (91%)
  local copies, waits for them, and re-layouts  8.33 us (7%)
  other arithmetic  1.54 us (1%)
    pallas_call x1, Pallas kernels, fused_call(): pl.pallas_call(functools.partial(fused_kernel, rows_dev, cols_dev, classe...  113 us
    unnamed x15, local copies, waits for them, and re-layouts  4.12 us

profile of v3, /device:TPU:1, one launch (start us, length us, event | category | flops | bytes accessed | tf_op | source)
XLA Modules:
  0.0 124.0 jit_solution(17748448972596001757)
XLA Ops:
  0.6 1.7 %copy_bitcast_fusion = (bf16[4,32,1,16,256]{4,3,2,1,0:T(8,128)(2,1)S(1)}, bf16[4,32,1,16,256]{4,3,2,1,0:T(8,128)(2,1)S(1)}) fusion(bf16[32,2,1,4,8,256]{5,4,3,1,0,2:T(8,128)(2,1)} %bitcast.16, bf16[32,2,1,4,8,256]{5,4,3,1,0,2:T(8,128)(2,1)} %bitcast.17), kind=kLoop, calls=%fused_computation.1 | loop fusion | bytes 4194304 | tf_op jit(solution)/shard_map/stack;reshape | solution.py:474
  2.4 1.5 %pad_maximum_fusion.x_ref = bf16[4,32,2,16,256]{4,3,2,1,0:T(8,128)(2,1)} fusion(bf16[4,32,1,16,256]{4,3,2,1,0:T(8,128)(2,1)S(1)} %get-tuple-element.18, bf16[4,32,1,16,256]{4,3,2,1,0:T(8,128)(2,1)S(1)} %get-tuple-element.19), kind=kLoop, calls=%fused_computation | loop fusion | flops 1048576 | bytes 4194304 | tf_op jit(solution)/shard_map/stack | solution.py:474
  3.9 113.5 %shard_map.118 = (bf16[4,32,16,256]{3,2,1,0:T(8,128)(2,1)}, f32[256,768]{1,0:T(8,128)}, f32[256,256]{1,0:T(8,128)}, f32[256,1024]{1,0:T(8,128)}, f32[1024,256]{1,0:T(8,128)}, /*index=5*/f32[2,256]{1,0:T(2,128)}) custom-call(bf16[4,32,2,16,256]{4,3,2,1,0:T(8,128)(2,1)} %pad_maximum_fusion.x_ref, bf16[256,768]{1,0:T(8,128)(2,1)} %wqkv.1, ...), custom_call_target="tpu_custom_call" | custom-call | tf_op jit(solution)/shard_map/pallas_call | solution.py:426
  117.4 0.0 copy-start.2
  117.4 0.0 copy-start.3
  117.4 0.0 copy-start.1
  117.4 2.5 %copy.15 = bf16[32,2,1,4,8,256]{5,4,3,1,0,2:T(8,128)(2,1)} copy(bf16[32,2,1,4,8,256]{5,4,1,0,3,2:T(8,128)(2,1)} %bitcast.15) | data formatting | bytes 2097152 | tf_op jit(solution)/shard_map/transpose | solution.py:472
  119.9 0.0 copy-done.2
  119.9 0.0 copy-start
  119.9 0.9 copy.23
  120.8 0.0 copy-done.3
  120.8 0.7 copy.24
  121.5 0.0 copy-done.1
  121.5 0.0 copy-start.4
  121.5 1.0 copy.25
  122.5 0.0 copy-done
  122.5 1.0 copy.26
  123.5 0.0 copy-done.4
  123.5 0.6 copy.27
Async XLA Ops:
  117.4 2.5 %copy-start.2 = (f32[256,768]{1,0:T(8,128)S(1)}, f32[256,768]{1,0:T(8,128)}, u32[]{:S(2)}) copy-start(f32[256,768]{1,0:T(8,128)} %get-tuple-element.27) | copy-start | bytes 2359300
  117.4 3.4 %copy-start.3 = (f32[256,256]{1,0:T(8,128)S(1)}, f32[256,256]{1,0:T(8,128)}, u32[]{:S(2)}) copy-start(f32[256,256]{1,0:T(8,128)} %get-tuple-element.28) | copy-start | bytes 786436
  117.4 4.1 %copy-start.1 = (f32[256,1024]{1,0:T(8,128)S(1)}, f32[256,1024]{1,0:T(8,128)}, u32[]{:S(2)}) copy-start(f32[256,1024]{1,0:T(8,128)} %get-tuple-element.29) | copy-start | bytes 3145732
  119.9 2.6 %copy-start = (f32[1024,256]{1,0:T(8,128)S(1)}, f32[1024,256]{1,0:T(8,128)}, u32[]{:S(2)}) copy-start(f32[1024,256]{1,0:T(8,128)} %get-tuple-element.30) | copy-start | bytes 3145732
  121.5 1.9 %copy-start.4 = (f32[2,256]{1,0:T(2,128)S(1)}, f32[2,256]{1,0:T(2,128)}, u32[]{:S(2)}) copy-start(f32[2,256]{1,0:T(2,128)} %get-tuple-element.31) | copy-start | bytes 6148
